TPU v7x, 128 devices: a whole 4x4x4 slice. The times are simulated.
128 devices in a mesh: dp: 8 (over y, core), tensor: 16 (over z, x).
Axes of the slice: x: 4, y: 4, z: 4, core: 2. Of those that a mesh axis runs over, the one named last changes fastest.
Arguments:
- mixer_input: bfloat16 [512, 8192], P('dp', 'tensor'), may hold values from -6 to 6
- gate_input: bfloat16 [512, 8192], P('dp', 'tensor'), may hold values from -6 to 6
- conv_state: bfloat16 [512, 3, 8192], P('dp', None, 'tensor'), may hold values from -6 to 6
- conv_weight: float32 [4, 8192], P(None, 'tensor'), may hold values from -3 to 3
- conv_bias: float32 [8192], P('tensor'), may hold values from -0.5 to 0.5
- state_proj: bfloat16 [8192, 288], P('tensor'), may hold values from -0.0625 to 0.0625
- step_proj: bfloat16 [256, 8192], P(None, 'tensor'), may hold values from -0.375 to 0.375
- step_bias: float32 [8192], P('tensor'), may hold values from -3 to 0
- decay_rate: float32 [16, 8192], P(None, 'tensor'), may hold values from 0.5 to 16
- skip_gain: float32 [8192], P('tensor'), may hold values from 0.5 to 1.5
- scan_state: float32 [512, 16, 8192], P('dp', None, 'tensor'), may hold values from -6 to 6
- output_proj: bfloat16 [8192, 4096], P('tensor'), may hold values from -0.09375 to 0.09375
- residual: bfloat16 [512, 4096], P('dp', 'tensor'), may hold values from -6 to 6
- router: bfloat16 [4096, 8], replicated, may hold values from -0.09375 to 0.09375
- expert_ids: int32 [512, 2], P('dp'), may hold values from 0 to 7, all different within a row; in each aligned block of 64 rows (0 to 63, 64 to 127, ...) at most 40 rows name the same one
- active: int32 [512], P('dp'), may hold values 0 or 1
- up_weight: bfloat16 [8, 4096, 14336], P('dp', None, 'tensor'), may hold values from -0.09375 to 0.09375
- down_weight: bfloat16 [8, 14336, 4096], P('dp', 'tensor'), may hold values from -0.0625 to 0.0625
Outputs:
- layer_out: bfloat16 [512, 4096], P('dp', 'tensor')
- state_out: float32 [512, 16, 8192], P('dp', None, 'tensor')
- conv_cache: bfloat16 [512, 3, 8192], P('dp', None, 'tensor')
Inputs may be any that keep to these rules, and one draw needn't show every extreme that they name: `expert_ids`: each row names two different experts; within each aligned block of 64 sessions (the sessions of one index of dp) no expert is named by more than 40 rows, a bound that some block reaches.
All inputs are finite; a program needn't handle non-finite values. No bound on the sum of `active` on one device may be relied on, other than what follows from the above.
Results may differ from a plain program's by a relative error of at most 0.02.
Values may be sent and summed in bfloat16 or wider, within the bound.
No kernel may reach another device: no remote copies, remote signals or barrier semaphores. Data moves between devices by JAX's collectives and lax.ppermute only.
A program may use at most 128 MiB of HBM per device.

v0:
```python
import jax
import jax.numpy as jnp
from jax import lax
from jax.sharding import PartitionSpec as P

DM = 4096
CAP = 40


def local(
    mixer_input,
    gate_input,
    conv_state,
    conv_weight,
    conv_bias,
    state_proj,
    step_proj,
    step_bias,
    decay_rate,
    skip_gain,
    scan_state,
    output_proj,
    residual,
    router,
    expert_ids,
    active,
    up_weight,
    down_weight,
):
    window = jnp.concatenate([conv_state, mixer_input[:, None, :]], axis=1)
    conv_sum = jnp.sum(window.astype(jnp.float32) * conv_weight[None], axis=1) + conv_bias
    conv_out = jax.nn.silu(conv_sum).astype(jnp.bfloat16)
    partial_proj = jnp.dot(conv_out, state_proj, preferred_element_type=jnp.float32)
    projected = lax.psum(partial_proj.astype(jnp.bfloat16), "tensor").astype(jnp.float32)
    low_rank = step_proj.shape[0]
    states = decay_rate.shape[0]
    step_raw = projected[:, :low_rank]
    input_map = projected[:, low_rank : low_rank + states]
    output_map = projected[:, low_rank + states :]
    step_norm = (
        step_raw * lax.rsqrt(jnp.mean(step_raw * step_raw, axis=1, keepdims=True) + 1e-06)
    ).astype(jnp.bfloat16)
    step_size = jax.nn.softplus(
        jnp.dot(step_norm, step_proj, preferred_element_type=jnp.float32) + step_bias
    )
    conv_float = conv_out.astype(jnp.float32)
    state_next = (
        jnp.exp(-step_size[:, None, :] * decay_rate[None]) * scan_state
        + (step_size * conv_float)[:, None, :] * input_map[:, :, None]
    )
    live_float = active.astype(jnp.float32)
    live_mask = active == 1
    scan_out = jnp.sum(output_map[:, :, None] * state_next, axis=1) + skip_gain * conv_float
    gated = (scan_out * jax.nn.silu(gate_input.astype(jnp.float32)) * live_float[:, None]).astype(
        jnp.bfloat16
    )
    state_out = jnp.where(live_mask[:, None, None], state_next, scan_state)
    conv_cache = jnp.where(live_mask[:, None, None], window[:, 1:, :], conv_state)
    experts_total = router.shape[1]
    sessions = expert_ids.shape[0]
    flat_ids = expert_ids.reshape(-1)
    one_hot = (flat_ids[:, None] == jnp.arange(experts_total, dtype=jnp.int32)[None, :]).astype(
        jnp.int32
    )
    slot_index = jnp.sum((jnp.cumsum(one_hot, axis=0) - one_hot) * one_hot, axis=1).reshape(
        sessions, 2
    )
    buffer_row = expert_ids * CAP + slot_index
    row_numbers = jnp.arange(experts_total * CAP, dtype=jnp.int32)
    placement = jnp.sum(
        ((buffer_row[None] == row_numbers[:, None, None]) & live_mask[None, :, None]).astype(
            jnp.float32
        ),
        axis=2,
    ).astype(jnp.bfloat16)
    slice_width = residual.shape[1]
    offset = lax.axis_index("tensor") * slice_width
    up_rows = up_weight[0]
    mixer_part = jnp.dot(gated, output_proj, preferred_element_type=jnp.float32)
    own_cols = lax.dynamic_slice_in_dim(mixer_part, offset, slice_width, 1) + residual.astype(
        jnp.float32
    )
    mixer_part = lax.dynamic_update_slice_in_dim(mixer_part, own_cols, offset, 1)
    hidden_sum = lax.psum(mixer_part.astype(jnp.bfloat16), "tensor").astype(jnp.float32)
    square_sum = jnp.sum(hidden_sum * hidden_sum, axis=1)
    raw_logits = jnp.dot(hidden_sum, router.astype(jnp.float32), precision=lax.Precision.HIGHEST)
    inv_rms = lax.rsqrt(square_sum / DM + 1e-06)
    hidden_local = lax.dynamic_slice_in_dim(hidden_sum, offset, slice_width, 1)
    normed = (hidden_sum * inv_rms[:, None]).astype(jnp.bfloat16)
    outgoing = jnp.dot(placement, normed, preferred_element_type=jnp.float32).astype(jnp.bfloat16)
    outgoing = outgoing.reshape(experts_total, CAP, normed.shape[1])
    incoming = lax.all_to_all(outgoing, "dp", split_axis=0, concat_axis=0, tiled=True)
    up_sum = jnp.dot(
        incoming.reshape(-1, incoming.shape[2]), up_rows, preferred_element_type=jnp.float32
    )
    hidden = jax.nn.silu(up_sum).astype(jnp.bfloat16)
    down_rows = down_weight[0]
    expert_share = lax.psum_scatter(
        lax.dot_general(
            down_rows, hidden, (((0,), (1,)), ((), ())), preferred_element_type=jnp.float32
        ).astype(jnp.bfloat16),
        "tensor",
        scatter_dimension=0,
        tiled=True,
    ).astype(jnp.float32)
    replies = expert_share.T.astype(jnp.bfloat16).reshape(-1, CAP, slice_width)
    returned = lax.all_to_all(replies, "dp", split_axis=0, concat_axis=0, tiled=True)
    gathered = returned.reshape(-1, slice_width)[buffer_row]
    chosen_logit = jnp.take_along_axis(raw_logits, expert_ids, axis=1) * inv_rms[:, None]
    first = 1.0 / (1.0 + jnp.exp(chosen_logit[:, 1] - chosen_logit[:, 0]))
    second = 1.0 / (1.0 + jnp.exp(chosen_logit[:, 0] - chosen_logit[:, 1]))
    route_weight = jnp.stack([first, second], axis=1) * live_float[:, None]
    layer_out = (
        hidden_local + jnp.sum(route_weight[:, :, None] * gathered.astype(jnp.float32), axis=1)
    ).astype(jnp.bfloat16)
    return (layer_out, state_out, conv_cache)


def solution(mesh):
    placed = (
        P("dp", "tensor"),
        P("dp", "tensor"),
        P("dp", None, "tensor"),
        P(None, "tensor"),
        P("tensor"),
        P("tensor", None),
        P(None, "tensor"),
        P("tensor"),
        P(None, "tensor"),
        P("tensor"),
        P("dp", None, "tensor"),
        P("tensor", None),
        P("dp", "tensor"),
        P(),
        P("dp", None),
        P("dp"),
        P("dp", None, "tensor"),
        P("dp", "tensor", None),
    )
    return jax.shard_map(
        local,
        mesh=mesh,
        in_specs=placed,
        out_specs=(P("dp", "tensor"), P("dp", None, "tensor"), P("dp", None, "tensor")),
        check_vma=False,
    )
```

profile of v0, /device:TPU:1, one launch (start us, length us, event | category | flops | bytes accessed | tf_op | source)
XLA Modules:
  0.0 320.1 jit_solution(11793327536139055235)
XLA Ops:
  7.2 1.2 multiply_reduce_fusion.2
  8.4 0.9 convolution_convert_fusion.1
  9.3 62.4 %psum.14 = bf16[64,288]{1,0:T(8,128)(2,1)S(1)} all-reduce(bf16[64,288]{1,0:T(8,128)(2,1)S(1)} %convolution_convert_fusion.1), channel_id=1, replica_groups=mesh['dp'=8,'tensor'=16] {'tensor'}, use_global_device_ids=true, to_apply=%region_1.2 | all-reduce | flops 18432 | bytes 73728 | tf_op jit(solution)/shard_map/psum | solution.py:34
  71.8 0.7 broadcast_compare_fusion
  72.5 0.7 convert_element_type.79
  73.2 1.3 fusion.39
  74.6 2.2 fusion.10
  76.8 0.7 copy-done.2
  77.5 0.9 fusion.28
  78.4 0.8 convert_element_type.82
  80.4 93.6 %all-reduce.2.cloned.1.call-done = bf16[64,4096]{1,0:T(8,128)(2,1)} async-done(((bf16[64,4096]{1,0:T(8,128)(2,1)}), bf16[64,4096]{1,0:T(8,128)(2,1)}) %all-reduce.2.cloned.1.call-update) | async-done | bytes 524304 | tf_op jit(solution)/shard_map/psum | solution.py:84
  174.1 1.2 multiply_reduce_fusion.1
  175.3 1.9 convolution_convert_fusion
  177.3 38.3 %all_to_all.10 = bf16[8,40,4096]{2,1,0:T(8,128)(2,1)S(1)} all-to-all(bf16[8,40,4096]{2,1,0:T(8,128)(2,1)S(1)} %bitcast.34), channel_id=1, replica_groups=mesh['dp'=8,'tensor'=16] {'dp'}, dimensions={0} | all-to-all | bytes 5242880 | tf_op jit(solution)/shard_map/all_to_all | solution.py:92
  215.6 12.3 %fusion.7 = bf16[4096,320]{0,1:T(8,128)(2,1)} fusion(bf16[1,896,4096]{2,1,0:T(8,128)(2,1)} %param.35, bf16[320,4096]{1,0:T(8,128)(2,1)S(1)} %bitcast.36, bf16[1,4096,896]{2,1,0:T(8,128)(2,1)} %param.34), kind=kOutput, calls=%fused_computation.8 | convolution fusion | flops 4700364800 | bytes 19922944 | tf_op jit(solution)/shard_map/dot_general | solution.py:99
  228.4 0.4 copy-done.4
  228.8 0.8 fusion.19
  229.6 0.2 fusion.41
  229.8 1.0 gather_fusion.1
  231.1 68.2 %reduce-scatter.2.cloned.1.call-done = bf16[256,320]{0,1:T(8,128)(2,1)} async-done(((bf16[4096,320]{0,1:T(8,128)(2,1)}), bf16[256,320]{0,1:T(8,128)(2,1)}) %reduce-scatter.2.cloned.1.call-update) | async-done | bytes 163856 | tf_op jit(solution)/shard_map/reduce_scatter | solution.py:98
  299.3 6.6 %all-to-all-start.1 = ((bf16[8,40,256]{2,1,0:T(8,128)(2,1)}), bf16[8,40,256]{2,1,0:T(8,128)(2,1)S(1)}, u32[]{:S(2)}, u32[]{:S(2)}) async-start(bf16[8,40,256]{2,1,0:T(8,128)(2,1)} %bitcast.39), calls=%async_computation.2 | async-start | bytes 327680 | tf_op jit(solution)/shard_map/all_to_all | solution.py:107
  306.1 5.4 %all-to-all-done.1 = bf16[8,40,256]{2,1,0:T(8,128)(2,1)S(1)} async-done(((bf16[8,40,256]{2,1,0:T(8,128)(2,1)}), bf16[8,40,256]{2,1,0:T(8,128)(2,1)S(1)}, u32[]{:S(2)}, u32[]{:S(2)}) %all-to-all-start.1) | async-done | bytes 163872 | tf_op jit(solution)/shard_map/all_to_all | solution.py:107
  311.5 0.8 gather_fusion
  312.6 0.6 add_convert_fusion
  (58 shorter events, 2.6 us)
Async XLA Ops:
  7.2 1.2 copy-start
  7.2 67.4 %copy-start.3 = (f32[64,16,512]{2,1,0:T(8,128)S(1)}, f32[64,16,512]{2,1,0:T(8,128)}, u32[]{:S(2)}) copy-start(f32[64,16,512]{2,1,0:T(8,128)} %param.28) | copy-start | bytes 6291460
  7.2 67.4 %copy-start.8 = (f32[16,512]{1,0:T(8,128)S(1)}, f32[16,512]{1,0:T(8,128)}, u32[]{:S(2)}) copy-start(f32[16,512]{1,0:T(8,128)} %param.26) | copy-start | bytes 98308
  7.2 166.9 %all-reduce.2.cloned.1.call-start = ((), (), s32[]{:S(2)}) async-start(), calls=%async_computation.3 | async-start | bytes 1048576 | tf_op jit(solution)/shard_map/psum | solution.py:84
  74.5 2.9 copy-start.2
  74.5 2.9 copy-start.6
  74.5 2.9 copy-start.11
  74.6 2.9 copy-start.12
  77.5 0.9 copy-start.9
  77.5 1.9 copy-start.10
  79.3 219.9 %reduce-scatter.2.cloned.1.call-start = ((), (), s32[]{:S(2)}) async-start(), calls=%async_computation.4 | async-start | bytes 2785280 | tf_op jit(solution)/shard_map/reduce_scatter | solution.py:98
  227.9 0.9 copy-start.4
  227.9 0.9 copy-start.5
  227.9 1.7 copy-start.1
  227.9 1.7 copy-start.7
  299.3 12.2 %all-to-all-start.1 = ((bf16[8,40,256]{2,1,0:T(8,128)(2,1)}), bf16[8,40,256]{2,1,0:T(8,128)(2,1)S(1)}, u32[]{:S(2)}, u32[]{:S(2)}) async-start(bf16[8,40,256]{2,1,0:T(8,128)(2,1)} %bitcast.39), calls=%async_computation.2 | async-start | bytes 327680 | tf_op jit(solution)/shard_map/all_to_all | solution.py:107
Sparse Core Ops, SparseCore 0:
  79.4 94.5 all-reduce.1
  228.0 71.1 reduce-scatter.1
where the time goes:
time: 321 us; the launch traced here: 320 us
  waiting for transfers between devices  167 us (52%)
  blocking collectives  101 us (31%)
  matrix products  17.6 us (5%)
  between operations  14.3 us (4%)
  other arithmetic  9.23 us (3%)
  starting transfers between devices  6.73 us (2%)
  local copies, waits for them, and re-layouts  4.34 us (1%)
    psum x1, waiting for transfers between devices, local(): lax.psum(mixer_part.astype(jnp.bfloat16), 'tensor').astype(jnp.float32)  93.6 us
    reduce_scatter x1, waiting for transfers between devices, local(): lax.psum_scatter(lax.dot_general(down_rows, hidden, (((0,), (1,)), ((), (...  68.2 us
    psum x1, blocking collectives, local(): lax.psum(partial_proj.astype(jnp.bfloat16), 'tensor').astype(jnp.float32)  62.4 us
    all_to_all x1, blocking collectives, local(): lax.all_to_all(outgoing, 'dp', split_axis=0, concat_axis=0, tiled=True)  38.3 us
    dot_general x1, matrix products, local(): lax.dot_general(down_rows, hidden, (((0,), (1,)), ((), ())), preferred_el...  12.3 us
    all_to_all x1, starting transfers between devices, local(): lax.all_to_all(replies, 'dp', split_axis=0, concat_axis=0, tiled=True)  6.65 us
  transfers between devices with their start and end apart: 3, of which 3 were waited for; matrix products, arithmetic and copies ran while one was open for 1% of the time, Pallas kernels for 0%

commit v1 on v0

v1 whole, which is shorter than its diff:
```python
import jax
import jax.numpy as jnp
from jax import lax
from jax.sharding import PartitionSpec as P

DM = 4096
CAP = 40
F32 = jnp.float32
BF16 = jnp.bfloat16


def sum_over_tensor(pieces):
    return jnp.sum(
        lax.all_to_all(pieces, "tensor", split_axis=0, concat_axis=0, tiled=True).astype(F32), axis=0
    )


def local(
    mixer_input,
    gate_input,
    conv_state,
    conv_weight,
    conv_bias,
    state_proj,
    step_proj,
    step_bias,
    decay_rate,
    skip_gain,
    scan_state,
    output_proj,
    residual,
    router,
    expert_ids,
    active,
    up_weight,
    down_weight,
):
    n_tensor = lax.axis_size("tensor")
    experts_total = router.shape[1]
    sessions = expert_ids.shape[0]
    slice_width = residual.shape[1]
    low_rank = step_proj.shape[0]
    states = decay_rate.shape[0]

    flat_ids = expert_ids.reshape(-1)
    pairs = jnp.arange(flat_ids.shape[0], dtype=jnp.int32)
    earlier = (flat_ids[:, None] == flat_ids[None, :]) & (pairs[None, :] < pairs[:, None])
    slot_index = jnp.sum(earlier.astype(jnp.int32), axis=1).reshape(sessions, 2)
    buffer_row = expert_ids * CAP + slot_index
    row_numbers = jnp.arange(experts_total * CAP, dtype=jnp.int32)
    live_float = active.astype(F32)
    live_mask = active == 1
    placement = jnp.any(
        (buffer_row[None] == row_numbers[:, None, None]) & live_mask[None, :, None], axis=2
    ).astype(BF16)

    window = jnp.concatenate([conv_state, mixer_input[:, None, :]], axis=1)
    conv_sum = jnp.sum(window.astype(F32) * conv_weight[None], axis=1) + conv_bias
    conv_out = jax.nn.silu(conv_sum).astype(BF16)
    partial_proj = jnp.dot(conv_out, state_proj, preferred_element_type=F32).astype(BF16)
    projected = sum_over_tensor(jnp.broadcast_to(partial_proj[None], (n_tensor,) + partial_proj.shape))
    step_raw = projected[:, :low_rank]
    input_map = projected[:, low_rank : low_rank + states]
    output_map = projected[:, low_rank + states :]
    step_norm = (
        step_raw * lax.rsqrt(jnp.mean(step_raw * step_raw, axis=1, keepdims=True) + 1e-06)
    ).astype(BF16)
    step_size = jax.nn.softplus(jnp.dot(step_norm, step_proj, preferred_element_type=F32) + step_bias)
    conv_float = conv_out.astype(F32)
    state_next = (
        jnp.exp(-step_size[:, None, :] * decay_rate[None]) * scan_state
        + (step_size * conv_float)[:, None, :] * input_map[:, :, None]
    )
    scan_out = jnp.sum(output_map[:, :, None] * state_next, axis=1) + skip_gain * conv_float
    gated = (scan_out * jax.nn.silu(gate_input.astype(F32)) * live_float[:, None]).astype(BF16)
    state_out = jnp.where(live_mask[:, None, None], state_next, scan_state)
    conv_cache = jnp.where(live_mask[:, None, None], window[:, 1:, :], conv_state)
    mixer_part = jnp.dot(gated, output_proj, preferred_element_type=F32).astype(BF16)
    hidden_local = sum_over_tensor(
        mixer_part.reshape(sessions, n_tensor, slice_width).transpose(1, 0, 2)
    ) + residual.astype(F32)

    outgoing = jnp.dot(placement, hidden_local.astype(BF16), preferred_element_type=F32).astype(BF16)
    incoming = lax.all_to_all(
        outgoing.reshape(experts_total, CAP, slice_width), "dp", split_axis=0, concat_axis=0, tiled=True
    ).reshape(experts_total * CAP, slice_width)
    columns = lax.all_to_all(
        jnp.broadcast_to(incoming[None], (n_tensor,) + incoming.shape),
        "tensor",
        split_axis=0,
        concat_axis=0,
        tiled=True,
    )
    rows = columns.transpose(1, 0, 2).reshape(experts_total * CAP, DM)
    rows_float = rows.astype(F32)
    inv_rms = lax.rsqrt(jnp.sum(rows_float * rows_float, axis=1) / DM + 1e-06)
    own_router = lax.dynamic_slice_in_dim(router, lax.axis_index("dp"), 1, 1)[:, 0].astype(F32)
    row_logit = jnp.sum(rows_float * own_router[None], axis=1) * inv_rms
    normed = (rows_float * inv_rms[:, None]).astype(BF16)
    up_sum = jnp.dot(normed, up_weight[0], preferred_element_type=F32)
    hidden = jax.nn.silu(up_sum).astype(BF16)
    expert_part = jnp.dot(hidden, down_weight[0], preferred_element_type=F32).astype(BF16)
    expert_share = sum_over_tensor(
        expert_part.reshape(experts_total * CAP, n_tensor, slice_width).transpose(1, 0, 2)
    ).astype(BF16)

    high = row_logit.astype(BF16)
    rest = row_logit - high.astype(F32)
    middle = rest.astype(BF16)
    low = (rest - middle.astype(F32)).astype(BF16)
    terms = jnp.stack([high, middle, low], axis=0).reshape(3, experts_total, CAP).transpose(1, 0, 2)
    terms = jnp.pad(terms, ((0, 0), (0, 5), (0, slice_width - CAP)))
    replies = jnp.concatenate([expert_share.reshape(experts_total, CAP, slice_width), terms], axis=1)
    returned = lax.all_to_all(replies, "dp", split_axis=0, concat_axis=0, tiled=True)
    returned_rows = returned[:, :CAP].reshape(experts_total * CAP, slice_width)
    returned_terms = returned[:, CAP : CAP + 3, :CAP].astype(F32)
    returned_logits = (
        returned_terms[:, 0] + (returned_terms[:, 1] + returned_terms[:, 2])
    ).reshape(-1)
    chosen = buffer_row.reshape(-1)[:, None] == row_numbers[None]
    gathered = jnp.dot(chosen.astype(BF16), returned_rows, preferred_element_type=F32).reshape(
        sessions, 2, slice_width
    )
    chosen_logit = jnp.sum(jnp.where(chosen, returned_logits[None], 0.0), axis=1).reshape(sessions, 2)
    first = 1.0 / (1.0 + jnp.exp(chosen_logit[:, 1] - chosen_logit[:, 0]))
    second = 1.0 / (1.0 + jnp.exp(chosen_logit[:, 0] - chosen_logit[:, 1]))
    route_weight = jnp.stack([first, second], axis=1) * live_float[:, None]
    layer_out = (hidden_local + jnp.sum(route_weight[:, :, None] * gathered, axis=1)).astype(BF16)
    return (layer_out, state_out, conv_cache)


def solution(mesh):
    placed = (
        P("dp", "tensor"),
        P("dp", "tensor"),
        P("dp", None, "tensor"),
        P(None, "tensor"),
        P("tensor"),
        P("tensor", None),
        P(None, "tensor"),
        P("tensor"),
        P(None, "tensor"),
        P("tensor"),
        P("dp", None, "tensor"),
        P("tensor", None),
        P("dp", "tensor"),
        P(),
        P("dp", None),
        P("dp"),
        P("dp", None, "tensor"),
        P("dp", "tensor", None),
    )
    return jax.shard_map(
        local,
        mesh=mesh,
        in_specs=placed,
        out_specs=(P("dp", "tensor"), P("dp", None, "tensor"), P("dp", None, "tensor")),
        check_vma=False,
    )
```

time: 321 us -> 176 us (0.55)
  blocking collectives: 101 us -> 12.6 us
  waiting for transfers between devices: 167 us -> 101 us
  starting transfers between devices: 6.73 us -> 25.9 us
  between operations: 14.3 us -> 0.97 us
  local copies, waits for them, and re-layouts: 4.34 us -> 9.62 us
    all_to_all x0 -> x4, waiting for transfers between devices: none -> 95.7 us  [the longest x3 57.7 us: sum_over_tensor(): lax.all_to_all(pieces, 'tensor', split_axis=0, concat_axis=0, tiled=True)]
    psum x1 -> x0, waiting for transfers between devices: 93.6 us -> none  [local(): lax.psum(mixer_part.astype(jnp.bfloat16), 'tensor').astype(jnp.float32)]
    reduce_scatter x1 -> x0, waiting for transfers between devices: 68.2 us -> none  [local(): lax.psum_scatter(lax.dot_general(down_rows, hidden, (((0,), (1,)), ((), (...]
    psum x1 -> x0, blocking collectives: 62.4 us -> none  [local(): lax.psum(partial_proj.astype(jnp.bfloat16), 'tensor').astype(jnp.float32)]
    all_to_all x1, blocking collectives: 38.3 us -> 12.6 us  [local(): lax.all_to_all(outgoing.reshape(experts_total, CAP, slice_width), 'dp', s...]
    all_to_all x0 -> x4, starting transfers between devices: none -> 19.7 us  [the longest x3 16 us: sum_over_tensor(): lax.all_to_all(pieces, 'tensor', split_axis=0, concat_axis=0, tiled=True)]
    reshape x2 -> x5, local copies, waits for them, and re-layouts: 0.21 us -> 4.72 us  [the longest x1 3.53 us: local(): expert_part.reshape(experts_total * CAP, n_tensor, slice_width)]
  transfers between devices with their start and end apart: 3 -> 5, of which waited for: 3 -> 5; matrix products, arithmetic and copies ran while one was open for 1% -> 2% of each run, Pallas kernels for 0% -> 0%
where the time goes in v1:
time: 176 us; the launch traced here: 175 us
  waiting for transfers between devices  101 us (57%)
  starting transfers between devices  25.9 us (15%)
  matrix products  16 us (9%)
  blocking collectives  12.6 us (7%)
  local copies, waits for them, and re-layouts  9.62 us (5%)
  other arithmetic  9.19 us (5%)
    all_to_all x3, waiting for transfers between devices, sum_over_tensor(): lax.all_to_all(pieces, 'tensor', split_axis=0, concat_axis=0, tiled=True)  57.7 us
    all_to_all x1, waiting for transfers between devices, local(): lax.all_to_all(jnp.broadcast_to(incoming[None], (n_tensor,) + incoming.sh...  38.1 us
    all_to_all x3, starting transfers between devices, sum_over_tensor(): lax.all_to_all(pieces, 'tensor', split_axis=0, concat_axis=0, tiled=True)  16 us
    all_to_all x1, blocking collectives, local(): lax.all_to_all(outgoing.reshape(experts_total, CAP, slice_width), 'dp', s...  12.6 us
    dot_general x1, matrix products, local(): jnp.dot(hidden, down_weight[0], preferred_element_type=F32).astype(BF16)  12.3 us
    all_to_all x1, starting transfers between devices, local(): lax.all_to_all(replies, 'dp', split_axis=0, concat_axis=0, tiled=True)  6.24 us
    all_to_all x1, waiting for transfers between devices, local(): lax.all_to_all(replies, 'dp', split_axis=0, concat_axis=0, tiled=True)  5.14 us
    all_to_all x1, starting transfers between devices, local(): lax.all_to_all(jnp.broadcast_to(incoming[None], (n_tensor,) + incoming.sh...  3.73 us
  transfers between devices with their start and end apart: 5, of which 5 were waited for; matrix products, arithmetic and copies ran while one was open for 2% of the time, Pallas kernels for 0%

profile of v1, /device:TPU:1, one launch (start us, length us, event | category | flops | bytes accessed | tf_op | source)
XLA Modules:
  0.0 175.2 jit_solution(5646022844144282727)
XLA Ops:
  0.7 1.0 multiply_reduce_fusion.1
  1.8 1.0 convolution_convert_fusion.2
  2.8 1.0 broadcast_in_dim.30
  3.8 8.4 %all-to-all-start = ((bf16[16,64,288]{2,1,0:T(8,128)(2,1)}), bf16[16,64,288]{2,1,0:T(8,128)(2,1)S(1)}, u32[]{:S(2)}, u32[]{:S(2)}) async-start(bf16[16,64,288]{2,1,0:T(8,128)(2,1)} %broadcast_in_dim.30), calls=%async_computation | async-start | bytes 1572864 | tf_op jit(solution)/shard_map/all_to_all | solution.py:14
  12.3 13.1 %all-to-all-done = bf16[16,64,288]{2,1,0:T(8,128)(2,1)S(1)} async-done(((bf16[16,64,288]{2,1,0:T(8,128)(2,1)}), bf16[16,64,288]{2,1,0:T(8,128)(2,1)S(1)}, u32[]{:S(2)}, u32[]{:S(2)}) %all-to-all-start) | async-done | bytes 589856 | tf_op jit(solution)/shard_map/all_to_all | solution.py:14
  25.7 1.2 fusion.48
  27.1 2.1 %fusion.11 = (f32[64,16,512]{2,1,0:T(8,128)}, f32[64,512]{1,0:T(8,128)S(1)}) fusion(f32[64,16,512]{2,1,0:T(8,128)S(1)} %copy-done.2, f32[64,16]{1,0:T(8,128)S(1)} %get-tuple-element.10, f32[64,512]{1,0:T(8,128)S(1)} %get-tuple-element.8, f32[16,512]{1,0:T(8,128)S(1)} %copy-done.7, f32[64,512]{1,0:T(8,128)S(1)} %get-tuple-element.7, ...), kind=kLoop, calls=%fused_computation.16 | loop fusion | flops 3637248 | bytes 4628544 | tf_op jit(solution)/shard_map/jit(_where)/select_n | solution.py:76
  30.0 0.9 convolution_convert_fusion
  30.9 0.8 copy.66
  31.7 3.8 %all-to-all-start.1 = ((bf16[16,64,256]{2,1,0:T(8,128)(2,1)}), bf16[16,64,256]{2,1,0:T(8,128)(2,1)S(1)}, u32[]{:S(2)}, u32[]{:S(2)}) async-start(bf16[16,64,256]{2,1,0:T(8,128)(2,1)} %bitcast.47), calls=%async_computation.1 | async-start | bytes 1048576 | tf_op jit(solution)/shard_map/all_to_all | solution.py:14
  36.3 8.9 %all-to-all-done.1 = bf16[16,64,256]{2,1,0:T(8,128)(2,1)S(1)} async-done(((bf16[16,64,256]{2,1,0:T(8,128)(2,1)}), bf16[16,64,256]{2,1,0:T(8,128)(2,1)S(1)}, u32[]{:S(2)}, u32[]{:S(2)}) %all-to-all-start.1) | async-done | bytes 524320 | tf_op jit(solution)/shard_map/all_to_all | solution.py:14
  45.6 12.6 %all_to_all.30 = bf16[8,40,256]{2,1,0:T(8,128)(2,1)S(1)} all-to-all(bf16[8,40,256]{2,1,0:T(8,128)(2,1)S(1)} %bitcast.53), channel_id=1, replica_groups=mesh['dp'=8,'tensor'=16] {'dp'}, dimensions={0} | all-to-all | bytes 327680 | tf_op jit(solution)/shard_map/all_to_all | solution.py:84
  58.3 1.8 %broadcast_in_dim.35 = bf16[16,320,256]{2,1,0:T(8,128)(2,1)} broadcast(bf16[320,256]{1,0:T(8,128)(2,1)S(1)} %bitcast.54), dimensions={1,2} | broadcast | bytes 2785280 | tf_op jit(solution)/shard_map/broadcast_in_dim | solution.py:88
  60.0 3.7 %all-to-all-start.3 = ((bf16[16,320,256]{2,1,0:T(8,128)(2,1)}), bf16[16,320,256]{2,1,0:T(8,128)(2,1)S(1)}, u32[]{:S(2)}, u32[]{:S(2)}) async-start(bf16[16,320,256]{2,1,0:T(8,128)(2,1)} %broadcast_in_dim.35), calls=%async_computation.3 | async-start | bytes 5242880 | tf_op jit(solution)/shard_map/all_to_all | solution.py:87
  63.8 0.9 convert_reduce_fusion.3
  64.7 38.1 %all-to-all-done.3 = bf16[16,320,256]{2,1,0:T(8,128)(2,1)S(1)} async-done(((bf16[16,320,256]{2,1,0:T(8,128)(2,1)}), bf16[16,320,256]{2,1,0:T(8,128)(2,1)S(1)}, u32[]{:S(2)}, u32[]{:S(2)}) %all-to-all-start.3) | async-done | bytes 2621472 | tf_op jit(solution)/shard_map/all_to_all | solution.py:87
  102.7 0.9 fusion.7
  103.7 0.9 fusion.10
  104.9 12.3 %fusion.4 = bf16[320,4096]{1,0:T(8,128)(2,1)} fusion(bf16[1,896,4096]{2,1,0:T(8,128)(2,1)} %param.35, bf16[320,4096]{1,0:T(8,128)(2,1)S(1)} %bitcast.49, bf16[1,4096,896]{2,1,0:T(8,128)(2,1)} %param.34), kind=kOutput, calls=%fused_computation.7 | convolution fusion | flops 4700364800 | bytes 19922944 | tf_op jit(solution)/shard_map/dot_general | solution.py:102
  117.2 3.5 %copy.65 = bf16[40,16,8,256]{3,2,0,1:T(8,128)(2,1)} copy(bf16[40,16,8,256]{3,2,1,0:T(8,128)(2,1)} %bitcast.50) | data formatting | bytes 5242880 | tf_op jit(solution)/shard_map/reshape | solution.py:104
  120.7 3.7 %all-to-all-start.4 = ((bf16[16,320,256]{2,1,0:T(8,128)(2,1)}), bf16[16,320,256]{2,1,0:T(8,128)(2,1)S(1)}, u32[]{:S(2)}, u32[]{:S(2)}) async-start(bf16[16,320,256]{2,1,0:T(8,128)(2,1)} %bitcast.48), calls=%async_computation.4 | async-start | bytes 5242880 | tf_op jit(solution)/shard_map/all_to_all | solution.py:14
  124.8 35.6 %all-to-all-done.4 = bf16[16,320,256]{2,1,0:T(8,128)(2,1)S(1)} async-done(((bf16[16,320,256]{2,1,0:T(8,128)(2,1)}), bf16[16,320,256]{2,1,0:T(8,128)(2,1)S(1)}, u32[]{:S(2)}, u32[]{:S(2)}) %all-to-all-start.4) | async-done | bytes 2621472 | tf_op jit(solution)/shard_map/all_to_all | solution.py:14
  161.5 6.2 %all-to-all-start.5 = ((bf16[8,48,256]{2,1,0:T(8,128)(2,1)}), bf16[8,48,256]{2,1,0:T(8,128)(2,1)S(1)}, u32[]{:S(2)}, u32[]{:S(2)}) async-start(bf16[8,48,256]{2,1,0:T(8,128)(2,1)} %fusion.21), calls=%async_computation.5 | async-start | bytes 393216 | tf_op jit(solution)/shard_map/all_to_all | solution.py:114
  168.5 5.1 %all-to-all-done.5 = bf16[8,48,256]{2,1,0:T(8,128)(2,1)S(1)} async-done(((bf16[8,48,256]{2,1,0:T(8,128)(2,1)}), bf16[8,48,256]{2,1,0:T(8,128)(2,1)S(1)}, u32[]{:S(2)}, u32[]{:S(2)}) %all-to-all-start.5) | async-done | bytes 196640 | tf_op jit(solution)/shard_map/all_to_all | solution.py:114
  (65 shorter events, 6.3 us)
Async XLA Ops:
  0.6 1.1 copy-start
  0.6 25.1 %copy-start.9 = (f32[512]{0:T(512)S(1)}, f32[512]{0:T(512)}, u32[]{:S(2)}) copy-start(f32[512]{0:T(512)} %param.22) | copy-start | bytes 6148
  0.7 11.6 %copy-start.12 = (s32[64]{0:T(128)S(1)}, s32[64]{0:T(128)}, u32[]{:S(2)}) copy-start(s32[64]{0:T(128)} %param.33) | copy-start | bytes 772
  0.7 25.1 %copy-start.11 = (f32[512]{0:T(512)S(1)}, f32[512]{0:T(512)}, u32[]{:S(2)}) copy-start(f32[512]{0:T(512)} %param.25) | copy-start | bytes 6148
  1.8 25.3 %copy-start.2 = (f32[64,16,512]{2,1,0:T(8,128)S(1)}, f32[64,16,512]{2,1,0:T(8,128)}, u32[]{:S(2)}) copy-start(f32[64,16,512]{2,1,0:T(8,128)} %param.28) | copy-start | bytes 6291460
  1.8 25.3 %copy-start.7 = (f32[16,512]{1,0:T(8,128)S(1)}, f32[16,512]{1,0:T(8,128)}, u32[]{:S(2)}) copy-start(f32[16,512]{1,0:T(8,128)} %param.26) | copy-start | bytes 98308
  3.8 21.6 %all-to-all-start = ((bf16[16,64,288]{2,1,0:T(8,128)(2,1)}), bf16[16,64,288]{2,1,0:T(8,128)(2,1)S(1)}, u32[]{:S(2)}, u32[]{:S(2)}) async-start(bf16[16,64,288]{2,1,0:T(8,128)(2,1)} %broadcast_in_dim.30), calls=%async_computation | async-start | bytes 1572864 | tf_op jit(solution)/shard_map/all_to_all | solution.py:14
  27.0 2.9 %copy-start.1 = (bf16[512,4096]{1,0:T(8,128)(2,1)S(1)}, bf16[512,4096]{1,0:T(8,128)(2,1)}, u32[]{:S(2)}) copy-start(bf16[512,4096]{1,0:T(8,128)(2,1)} %param.29) | copy-start | bytes 12582916
  27.0 2.9 %copy-start.6 = (bf16[64,512]{1,0:T(8,128)(2,1)S(1)}, bf16[64,512]{1,0:T(8,128)(2,1)}, u32[]{:S(2)}) copy-start(bf16[64,512]{1,0:T(8,128)(2,1)} %param.19) | copy-start | bytes 196612
  27.0 2.9 %copy-start.10 = (f32[512]{0:T(512)S(1)}, f32[512]{0:T(512)}, u32[]{:S(2)}) copy-start(f32[512]{0:T(512)} %param.27) | copy-start | bytes 6148
  30.0 5.6 %copy-start.8 = (s32[64,2]{0,1:T(2,128)S(1)}, s32[64,2]{0,1:T(2,128)}, u32[]{:S(2)}) copy-start(s32[64,2]{0,1:T(2,128)} %param.32) | copy-start | bytes 1540
  30.9 14.5 %copy-start.5 = (bf16[64,256]{1,0:T(8,128)(2,1)S(1)}, bf16[64,256]{1,0:T(8,128)(2,1)}, u32[]{:S(2)}) copy-start(bf16[64,256]{1,0:T(8,128)(2,1)} %param.30) | copy-start | bytes 98308
  31.7 13.6 %all-to-all-start.1 = ((bf16[16,64,256]{2,1,0:T(8,128)(2,1)}), bf16[16,64,256]{2,1,0:T(8,128)(2,1)S(1)}, u32[]{:S(2)}, u32[]{:S(2)}) async-start(bf16[16,64,256]{2,1,0:T(8,128)(2,1)} %bitcast.47), calls=%async_computation.1 | async-start | bytes 1048576 | tf_op jit(solution)/shard_map/all_to_all | solution.py:14
  60.0 42.7 %all-to-all-start.3 = ((bf16[16,320,256]{2,1,0:T(8,128)(2,1)}), bf16[16,320,256]{2,1,0:T(8,128)(2,1)S(1)}, u32[]{:S(2)}, u32[]{:S(2)}) async-start(bf16[16,320,256]{2,1,0:T(8,128)(2,1)} %broadcast_in_dim.35), calls=%async_computation.3 | async-start | bytes 5242880 | tf_op jit(solution)/shard_map/all_to_all | solution.py:87
  120.7 39.7 %all-to-all-start.4 = ((bf16[16,320,256]{2,1,0:T(8,128)(2,1)}), bf16[16,320,256]{2,1,0:T(8,128)(2,1)S(1)}, u32[]{:S(2)}, u32[]{:S(2)}) async-start(bf16[16,320,256]{2,1,0:T(8,128)(2,1)} %bitcast.48), calls=%async_computation.4 | async-start | bytes 5242880 | tf_op jit(solution)/shard_map/all_to_all | solution.py:14
  124.4 43.3 %copy-start.3 = (bf16[64,3,512]{2,0,1:T(8,128)(2,1)S(1)}, bf16[64,3,512]{2,0,1:T(8,128)(2,1)}, u32[]{:S(2)}) copy-start(bf16[64,3,512]{2,0,1:T(8,128)(2,1)} %param.20) | copy-start | bytes 589828
  124.4 43.3 %copy-start.4 = (bf16[64,512]{1,0:T(8,128)(2,1)S(1)}, bf16[64,512]{1,0:T(8,128)(2,1)}, u32[]{:S(2)}) copy-start(bf16[64,512]{1,0:T(8,128)(2,1)} %param.18) | copy-start | bytes 196612
  161.5 12.1 %all-to-all-start.5 = ((bf16[8,48,256]{2,1,0:T(8,128)(2,1)}), bf16[8,48,256]{2,1,0:T(8,128)(2,1)S(1)}, u32[]{:S(2)}, u32[]{:S(2)}) async-start(bf16[8,48,256]{2,1,0:T(8,128)(2,1)} %fusion.21), calls=%async_computation.5 | async-start | bytes 393216 | tf_op jit(solution)/shard_map/all_to_all | solution.py:114
